TPU v7x, 256 devices: a whole 4x4x8 slice. The times are simulated.
256 devices in a mesh: ka: 64 (over y, x, z_lo), ga: 4 (over z_hi, core).
Axes of the slice: x: 4, y: 4, z: 8 (z_hi: 2, z_lo: 4; z = z_hi * 4 + z_lo), core: 2. Of those that a mesh axis runs over, the one named last changes fastest.
Arguments:
- density: bfloat16 [128, 2, 64, 1024], P('ka', None, None, 'ga'), may hold values from -1.75 to 1.75
- partner: int32 [128], replicated, may hold values from 0 to 127, as said below
- qindex: int32 [128, 128], P('ka'), may hold values from 0 to 7
- gshift: int32 [128, 1024], P('ka'), may hold values from 0 to 1023, each once within a row
- screened: bfloat16 [8, 2, 1024, 1024], P(None, None, None, 'ga'), may hold values from -0.1875 to 0.1875
- coulomb: float32 [1024], P('ga'), may hold values from 0.25 to 2
Outputs:
- coupling: bfloat16 [128, 128, 2, 4096], P('ga', 'ka')
Inputs may be any that keep to these rules, and one draw needn't show every extreme that they name: partner[partner[k]] = k and partner[k] != k.
All inputs are finite; a program needn't handle non-finite values.
Results may differ from a plain program's by a relative error of at most 0.0049.
Values may be sent and summed in bfloat16 or wider, within the bound.
A program may use at most 128 MiB of HBM per device.

v0:
```python
import jax
import jax.numpy as jnp
from jax import lax
from jax.sharding import PartitionSpec as P


def conjugate(picked):
    return jnp.concatenate([picked[:, :1], -picked[:, 1:]], axis=1)


def contract_rows(kernel, cols, qcols, pairs):
    count = cols.shape[0]
    pieces = []
    for row in range(kernel.shape[0]):
        chosen = jnp.take(kernel[row], qcols[row], axis=0)
        block = jnp.einsum("jcpg,jdrg->jcdpr", chosen, cols, preferred_element_type=jnp.float32)
        b_re = block[:, 0, 0] - block[:, 1, 1]
        b_im = block[:, 0, 1] + block[:, 1, 0]
        pieces.append(jnp.stack([b_re, b_im], axis=1).reshape(count, 2, pairs * pairs))
    return jnp.stack(pieces, axis=1)


def on_device(density, partner, qindex, gshift, screened, coulomb):
    pairs = density.shape[2]
    block_width = density.shape[3]
    whole_rows = lax.all_gather(density, "ga", axis=3, tiled=True)
    shifted = jax.vmap(lambda row, order: jnp.take(row, order, axis=2))(whole_rows, gshift)
    prod = jnp.einsum("kcpg,qdgh->kqcdph", shifted, screened, preferred_element_type=jnp.float32)
    x_re = prod[:, :, 0, 0] - prod[:, :, 1, 1]
    x_im = prod[:, :, 0, 1] + prod[:, :, 1, 0]
    product = jnp.stack([x_re, x_im], axis=2)
    start_g = lax.axis_index("ga") * block_width
    local_part = lax.dynamic_slice_in_dim(shifted, start_g, block_width, 3).astype(jnp.float32)
    kernel = (2.0 * coulomb * local_part[:, None] - product).astype(jnp.bfloat16)
    initials = lax.all_gather(density, "ka", axis=0, tiled=True)
    columns = conjugate(jnp.take(initials, partner, axis=0))
    summed = lax.psum_scatter(
        contract_rows(kernel, columns, qindex, pairs), "ga", scatter_dimension=0, tiled=True
    )
    return summed.astype(jnp.bfloat16)


def solution(mesh):
    return jax.shard_map(
        on_device,
        mesh=mesh,
        in_specs=(
            P("ka", None, None, "ga"),
            P(),
            P("ka", None),
            P("ka", None),
            P(None, None, None, "ga"),
            P("ga"),
        ),
        out_specs=P("ga", "ka", None, None),
        check_vma=False,
    )
```

profile of v0, /device:TPU:32, one launch (start us, length us, event | category | flops | bytes accessed | tf_op | source)
XLA Modules:
  0.0 791.2 jit_solution(18260203590898797736)
XLA Ops:
  7.3 1.1 copy.21
  9.1 21.3 %all_gather.7 = bf16[2,2,64,1024]{2,1,3,0:T(2,128)(2,1)S(1)} all-gather(bf16[2,2,64,256]{2,1,3,0:T(2,128)(2,1)S(1)} %copy.21), channel_id=1, replica_groups=mesh['ka'=64,'ga'=4] {'ga'}, dimensions={3}, use_global_device_ids=true | all-gather | bytes 655360 | tf_op jit(solution)/shard_map/all_gather | solution.py:26
  30.4 8.5 %gather_fusion.1 = bf16[2048,2,64]{2,1,0:T(2,128)(2,1)S(1)} fusion(bf16[2,2,64,1024]{2,1,3,0:T(2,128)(2,1)S(1)} %all_gather.7, s32[2048]{0:T(1024)S(1)} %bitcast.80), kind=kCustom, calls=%fused_computation.3 | custom fusion | bytes 1064960 | tf_op jit(solution)/shard_map/vmap(jit(_take))/gather | solution.py:27
  39.0 0.7 copy.22
  39.7 0.8 compare_and_fusion.2
  41.9 5.8 fusion.10
  48.5 6.5 gather_fusion.2
  55.0 6.5 gather_fusion.3
  62.8 329.4 %all-gather.2.cloned.1.call-done = bf16[128,2,64,256]{3,2,1,0:T(8,128)(2,1)} async-done(((bf16[2,2,64,256]{3,2,1,0:T(8,128)(2,1)}), bf16[128,2,64,256]{3,2,1,0:T(8,128)(2,1)}) %all-gather.2.cloned.1.call-update) | async-done | bytes 8388624 | tf_op jit(solution)/shard_map/all_gather | solution.py:35
  392.2 10.0 %gather_fusion = bf16[128,2,64,256]{3,2,1,0:T(8,128)(2,1)} fusion(bf16[128,2,64,256]{3,2,1,0:T(8,128)(2,1)} %all-gather.2.cloned.1.call-done, s32[1024]{0:T(1024)S(1)} %pad_clamp_fusion.2), kind=kCustom, calls=%fused_computation.2 | custom fusion | bytes 16777728 | tf_op jit(solution)/shard_map/jit(_take)/gather | solution.py:36
  402.2 7.6 broadcast_select_fusion
  409.7 6.6 fusion.23
  417.0 10.3 %convolution_bitcast_fusion.1 = f32[128,2,2,64,64]{3,4,1,2,0:T(8,128)} fusion(bf16[128,2,64,256]{3,2,1,0:T(8,128)(2,1)S(1)} %bitcast.82, pred[128]{0:T(512)(128)(4,1)S(1)} %get-tuple-element.6, bf16[128,1,64,256]{3,2,1,0:T(8,128)(2,1)} %get-tuple-element.15, bf16[128,1,64,256]{3,2,1,0:T(8,128)(2,1)} %get-tuple-element.14), kind=kOutput, calls=%fused_computation.5 | convolution fusion | flops 1094713344 | bytes 25165952 | tf_op jit(solution)/shard_map/jcpg,jdrg->jcdpr/dot_general | solution.py:16
  427.3 12.1 %slice_subtract_fusion.1 = (f32[128,1,1,64,64]{3,4,1,2,0:T(8,128)}, f32[128,1,1,64,64]{3,4,1,2,0:T(8,128)}) fusion(f32[128,2,2,64,64]{3,4,1,2,0:T(8,128)} %convolution_bitcast_fusion.1), kind=kLoop, calls=%fused_computation.20 | loop fusion | flops 1048576 | bytes 12582912 | tf_op jit(solution)/shard_map/sub | solution.py:17
  439.4 4.5 copy.26
  443.9 5.4 copy.27
  449.3 11.6 %convolution_bitcast_fusion = f32[128,2,2,64,64]{3,4,1,2,0:T(8,128)} fusion(bf16[128,2,64,256]{3,2,1,0:T(8,128)(2,1)} %gather_fusion.3, pred[128]{0:T(512)(128)(4,1)S(1)} %get-tuple-element.18, bf16[128,1,64,256]{3,2,1,0:T(8,128)(2,1)} %get-tuple-element.15, bf16[128,1,64,256]{3,2,1,0:T(8,128)(2,1)} %get-tuple-element.14), kind=kOutput, calls=%fused_computation.4 | convolution fusion | flops 1094713344 | bytes 25165952 | tf_op jit(solution)/shard_map/jcpg,jdrg->jcdpr/dot_general | solution.py:16
  460.9 12.1 %slice_subtract_fusion = (f32[128,1,1,64,64]{3,4,1,2,0:T(8,128)}, f32[128,1,1,64,64]{3,4,1,2,0:T(8,128)}) fusion(f32[128,2,2,64,64]{3,4,1,2,0:T(8,128)} %convolution_bitcast_fusion), kind=kLoop, calls=%fused_computation.18 | loop fusion | flops 1048576 | bytes 12582912 | tf_op jit(solution)/shard_map/sub | solution.py:17
  472.9 5.3 copy.28
  478.2 5.3 copy.29
  483.6 5.4 maximum_maximum_fusion
  489.0 13.2 %copy.30 = f32[128,2,2,4096]{3,2,1,0:T(2,128)} copy(f32[128,2,2,4096]{0,3,2,1:T(8,128)} %maximum_maximum_fusion) | data formatting | bytes 16777216 | tf_op jit(solution)/shard_map/stack | solution.py:20
  502.2 278.7 %all-reduce.2 = bf16[128,2,2,4096]{3,2,1,0:T(2,128)(2,1)} all-reduce(f32[128,2,2,4096]{3,2,1,0:T(2,128)} %copy.30), channel_id=2, replica_groups=mesh['ka'=64,'ga'=4] {'ga'}, use_global_device_ids=true, to_apply=%region_0.0.clone | all-reduce | flops 2097152 | bytes 12582912
  780.9 3.5 dynamic-slice_convert_fusion
  (25 shorter events, 4.8 us)
Async XLA Ops:
  6.5 385.7 %all-gather.2.cloned.1.call-start = ((), (), s32[]{:S(2)}) async-start(), calls=%async_computation | async-start | bytes 8519680 | tf_op jit(solution)/shard_map/all_gather | solution.py:35
  55.0 6.5 copy-start.1
  55.0 7.8 copy-start
  402.2 14.2 %slice-start = ((s8[8388608]{0:T(1024)(128)(4,1)}), s8[4194304]{0:T(1024)(128)(4,1)S(1)}, s32[]{:S(2)}) async-start(s8[8388608]{0:T(1024)(128)(4,1)} %bitcast.81), calls=%async_computation.1 | async-start | bytes 8388608
  409.7 7.2 slice-start.1
Sparse Core Ops, SparseCore 0:
  9.1 383.0 all-gather.1
where the time goes:
time: 797 us; the launch traced here: 791 us
  waiting for transfers between devices  330 us (41%)
  blocking collectives  300 us (38%)
  local copies, waits for them, and re-layouts  71.9 us (9%)
  other arithmetic  47.3 us (6%)
  matrix products  27.7 us (3%)
  between operations  14.2 us (2%)
    all_gather x1, waiting for transfers between devices, on_device(): initials = lax.all_gather(density, 'ka', axis=0, tiled=True)  329 us
    unnamed x1, blocking collectives  279 us
    sub x2, other arithmetic, contract_rows(): b_re = block[:, 0, 0] - block[:, 1, 1]  24.2 us
    dot_general x2, matrix products, contract_rows(): jnp.einsum('jcpg,jdrg->jcdpr', chosen, cols, preferred_element_type=jnp.f...  21.9 us
    all_gather x1, blocking collectives, on_device(): whole_rows = lax.all_gather(density, 'ga', axis=3, tiled=True)  21.3 us
  transfers between devices with their start and end apart: 1, of which 1 were waited for; matrix products, arithmetic and copies ran while one was open for 4% of the time, Pallas kernels for 0%

commit v1 on v0

v1 whole, which is shorter than its diff:
```python
import functools

import jax
import jax.numpy as jnp
from jax import lax
from jax.experimental import pallas as pl
from jax.experimental.pallas import tpu as pltpu
from jax.sharding import PartitionSpec as P

MESH = pl.DeviceIdType.MESH
F32, BF16 = jnp.float32, jnp.bfloat16
PAIRS, NG, NQ, NKR, WIDTH = 64, 1024, 8, 128, 256
CHUNKS = 8
RC = PAIRS // CHUNKS
BLOCK = NKR // 4
GROUPS = ((0, 1), (1, 3), (3, 8))
NT = (((1,), (1,)), ((), ()))


def dot(a, b):
    return jnp.dot(a, b, preferred_element_type=F32)


def dot_nt(a, b):
    return lax.dot_general(a, b, NT, preferred_element_type=F32)


def kernel(density, partner, qindex, gshift, screened, coulomb, out,
           D, SG, OH, SH, W, KA, KB, res, xsend, xrecv, keepx, fin, csend, crecv,
           wsem, s_s, s_r, z_s, z_r, a1_s, a1_r, a2_s, a2_r, b1_s, b1_r, b2_s, b2_r, x_s, x_r, c_s, c_r):
    ka, ga = lax.axis_index("ka"), lax.axis_index("ga")
    y, x, z = ka // 16, (ka // 4) % 4, ka % 4
    half, core = ga // 2, ga % 2
    ym, yp, yo = (y + 3) % 4, (y + 1) % 4, (y + 2) % 4
    xm, xp, xo = (x + 3) % 4, (x + 1) % 4, (x + 2) % 4

    def at(yy, xx, zz):
        return (yy * 16 + xx * 4 + zz, ga)

    mate_ga = half * 2 + (1 - core)
    cross_ga = (1 - half) * 2 + core
    far_ga = (1 - half) * 2 + (1 - core)
    mate, cross = (ka, mate_ga), (ka, cross_ga)
    line = [at(y, x, (z + d) % 4) for d in (1, 2, 3)]
    ring = [at(y, xp, z), at(y, xm, z), at(yp, x, z), at(ym, x, z)]
    ring_b = [ring[2], ring[3], ring[0], ring[1]]

    def rc(src, dst, ss, rs, dev):
        return pltpu.make_async_remote_copy(
            src_ref=src, dst_ref=dst, send_sem=ss, recv_sem=rs, device_id=dev, device_id_type=MESH)

    def got(land, ss, rs, dev):
        rc(land, land, ss, rs, dev).wait_recv()

    def sent(src, ss, rs, dev):
        rc(src, src, ss, rs, dev).wait_send()

    barrier = pltpu.get_barrier_semaphore()
    for peer in line + ring + [mate, cross]:
        pl.semaphore_signal(barrier, inc=1, device_id=peer, device_id_type=MESH)
    wcopy = pltpu.make_async_copy(screened, W, wsem)
    wcopy.start()

    for h in range(2):
        both = [density[j, h].astype(F32).reshape(CHUNKS, RC, WIDTH) for j in range(2)]
        D[h, :, y, x, z] = jnp.concatenate(both, axis=1).astype(BF16)
    SG[ga] = density[...]
    pl.semaphore_wait(barrier, 9)

    s_parts = [(SG.at[ga], mate), (SG.at[ga], cross), (SG.at[cross_ga], mate)]
    s_land = [SG.at[mate_ga], SG.at[cross_ga], SG.at[far_ga]]

    def s_send(i):
        rc(s_parts[i][0], s_parts[i][0], s_s.at[i], s_r.at[i], s_parts[i][1]).start()

    def s_got(i):
        got(s_land[i], s_s.at[i], s_r.at[i], s_parts[i][1])

    def z_part(g, zz):
        lo, hi = GROUPS[g]
        return D.at[:, lo:hi, y, x, zz]

    def z_send(g):
        for d in range(3):
            rc(z_part(g, z), z_part(g, z), z_s.at[g, d], z_r.at[g, d], line[d]).start()

    def z_got(g):
        for d in range(3):
            got(z_part(g, (z + 3 - d) % 4), z_s.at[g, d], z_r.at[g, d], line[d])

    def a1_src(c):
        return [D.at[0, c, y, x], D.at[0, c, y, x], D.at[1, c, y, x], D.at[1, c, y, x]]

    def a1_land(c):
        return [D.at[0, c, y, xm], D.at[0, c, y, xp], D.at[1, c, ym, x], D.at[1, c, yp, x]]

    def a2_src(c):
        return [D.at[0, c, y, xm, 0:2], D.at[0, c, y, xp, 2:4], D.at[1, c, ym, x, 0:2], D.at[1, c, yp, x, 2:4]]

    def a2_land(c):
        return [D.at[0, c, y, xo, 0:2], D.at[0, c, y, xo, 2:4], D.at[1, c, yo, x, 0:2], D.at[1, c, yo, x, 2:4]]

    def b1_src(c):
        return [D.at[0, c, y], D.at[0, c, y], D.at[1, c, :, x], D.at[1, c, :, x]]

    def b1_land(c):
        return [D.at[0, c, ym], D.at[0, c, yp], D.at[1, c, :, xm], D.at[1, c, :, xp]]

    def b2_src(c):
        return [D.at[0, c, ym, 0:2], D.at[0, c, yp, 2:4], D.at[1, c, 0:2, xm], D.at[1, c, 2:4, xp]]

    def b2_land(c):
        return [D.at[0, c, yo, 0:2], D.at[0, c, yo, 2:4], D.at[1, c, 0:2, xo], D.at[1, c, 2:4, xo]]

    phases = {
        "a1": (a1_src, a1_land, a1_s, a1_r, ring),
        "a2": (a2_src, a2_land, a2_s, a2_r, ring),
        "b1": (b1_src, b1_land, b1_s, b1_r, ring_b),
        "b2": (b2_src, b2_land, b2_s, b2_r, ring_b),
    }

    def send(name, c):
        src, _, ss, rs, to = phases[name]
        for i, part in enumerate(src(c)):
            rc(part, part, ss.at[c, i], rs.at[c, i], to[i]).start()

    def recv(name, c):
        _, land, ss, rs, to = phases[name]
        for i, part in enumerate(land(c)):
            got(part, ss.at[c, i], rs.at[c, i], to[i])

    def done(name, c):
        src, _, ss, rs, to = phases[name]
        for i, part in enumerate(src(c)):
            sent(part, ss.at[c, i], rs.at[c, i], to[i])

    def shift_part(b, first):
        rows = pl.ds(pl.multiple_of(b * WIDTH, WIDTH), WIDTH)
        for j in range(2):
            term = dot(SG[b, j].reshape(2 * PAIRS, WIDTH), OH[j, rows, :])
            if first:
                SH[j] = term.astype(BF16)
            else:
                SH[j] = (SH[j].astype(F32) + term).astype(BF16)

    s_send(1)
    s_send(0)
    z_send(0)

    def build(t, _):
        rows = pl.ds(pl.multiple_of(t * 64, 64), 64)
        index = lax.broadcasted_iota(jnp.int32, (64, NG), 0) + t * 64
        for j in range(2):
            OH[j, rows, :] = jnp.where(index == gshift[j:j + 1, :], 1.0, 0.0).astype(BF16)
        return 0

    lax.fori_loop(0, NG // 64, build, 0)

    z_got(0)
    send("a1", 0)
    z_send(1)
    recv("a1", 0)
    send("a2", 0)
    z_send(2)
    s_got(0)
    shift_part(ga, True)
    shift_part(mate_ga, False)
    recv("a2", 0)
    send("b1", 0)
    z_got(1)
    send("a1", 1)
    send("a1", 2)
    s_got(1)
    s_send(2)
    shift_part(cross_ga, False)
    recv("a1", 1)
    send("a2", 1)
    recv("b1", 0)
    send("b2", 0)
    recv("a1", 2)
    send("a2", 2)
    recv("a2", 1)
    send("b1", 1)
    z_got(2)
    send("a1", 3)
    s_got(2)
    shift_part(far_ga, False)
    wcopy.wait()

    local = pl.ds(pl.multiple_of(ga * WIDTH, WIDTH), WIDTH)

    def screen(q, _):
        rows = SH[...].reshape(4 * PAIRS, NG)
        by_re, by_im = dot(rows, W[q, 0]), dot(rows, W[q, 1])
        twice = 2.0 * coulomb[...]
        a, b = [], []
        for j in range(2):
            re, im = slice(j * 128, j * 128 + 64), slice(j * 128 + 64, j * 128 + 128)
            own = SH[j, :, local].astype(F32)
            k_re = (twice * own[:64] - (by_re[re] - by_im[im])).astype(BF16)
            k_im = (twice * own[64:] - (by_im[re] + by_re[im])).astype(BF16)
            a += [k_re, k_im]
            b += [k_im, -k_re]
        KA[q] = jnp.concatenate(a, axis=0)
        KB[q] = jnp.concatenate(b, axis=0)
        return 0

    lax.fori_loop(0, NQ, screen, 0)

    def multiply(c, q_lo, q_hi):
        def one(q, _):
            for t in range(4):
                d_re = D[0, c, t].reshape(256, WIDTH)
                d_im = D[1, c, t].reshape(256, WIDTH)
                both = dot_nt(d_re, KA[q]) + dot_nt(d_im, KB[q])
                for k in range(2):
                    res[k, q, t * 32:(t + 1) * 32] = both[:, k * 128:(k + 1) * 128].reshape(32, RC, 128)
            return 0

        lax.fori_loop(q_lo, q_hi, one, 0)

    def pick(block, put):
        def one(i, _):
            col = block * BLOCK + i
            m = partner[col]
            for k in range(2):
                put(i, k, res[k, qindex[k, col], m])
            return 0

        lax.fori_loop(0, BLOCK, one, 0, unroll=4)

    def x_send(c, part):
        rc(xsend.at[c, part], xrecv.at[c, part], x_s.at[c, part], x_r.at[c, part], mate).start()

    def x_got(c, part):
        got(xrecv.at[c, part], x_s.at[c, part], x_r.at[c, part], mate)

    def settle(c):
        def put_far(i, k, v):
            xsend[c, 0, i, k] = v

        def put_mate(i, k, v):
            xsend[c, 1, i, k] = v

        def put_cross(i, k, v):
            keepx[i, k] = v

        def put_own(i, k, v):
            fin[c, i, k] = v

        pick(far_ga, put_far)
        x_send(c, 0)
        pick(mate_ga, put_mate)
        x_send(c, 1)
        pick(cross_ga, put_cross)
        pick(ga, put_own)
        x_got(c, 0)
        total = keepx[...] + xrecv[c, 0]
        csend[c] = total.reshape(BLOCK, 2 * RC, 128).astype(BF16)
        rc(csend.at[c], crecv.at[c], c_s.at[c], c_r.at[c], cross).start()
        x_got(c, 1)
        fin[c] = fin[c] + xrecv[c, 1]

    def finish(c):
        got(crecv.at[c], c_s.at[c], c_r.at[c], cross)
        total = fin[c].reshape(BLOCK, 2 * RC, 128) + crecv[c].astype(F32)
        out[:, c] = total.astype(BF16)

    def tick(c, _):
        @pl.when(c + 2 < CHUNKS)
        def _():
            recv("a2", c + 2)
            send("b1", c + 2)

        recv("b2", c)
        multiply(c, 0, NQ // 2)

        @pl.when(c + 1 < CHUNKS)
        def _():
            recv("b1", c + 1)
            send("b2", c + 1)

        @pl.when(c + 3 < CHUNKS)
        def _():
            recv("a1", c + 3)
            send("a2", c + 3)

        @pl.when(c + 4 < CHUNKS)
        def _():
            send("a1", c + 4)

        multiply(c, NQ // 2, NQ)
        settle(c)

        @pl.when(c >= 3)
        def _():
            finish(c - 3)

        return 0

    lax.fori_loop(0, CHUNKS, tick, 0)

    def last(c, _):
        for name in phases:
            done(name, c)
        for part in range(2):
            sent(xsend.at[c, part], x_s.at[c, part], x_r.at[c, part], mate)
        sent(csend.at[c], c_s.at[c], c_r.at[c], cross)
        return 0

    lax.fori_loop(0, CHUNKS, last, 0)
    for i in range(3):
        sent(s_parts[i][0], s_s.at[i], s_r.at[i], s_parts[i][1])
    for g in range(3):
        for d in range(3):
            sent(z_part(g, z), z_s.at[g, d], z_r.at[g, d], line[d])
    for c in range(CHUNKS - 3, CHUNKS):
        finish(c)


def on_device(density, partner, qindex, gshift, screened, coulomb):
    vmem = pl.BlockSpec(memory_space=pltpu.VMEM)
    smem = pl.BlockSpec(memory_space=pltpu.SMEM)
    dma = pltpu.SemaphoreType.DMA
    ring_sems = [dma((CHUNKS, 4))] * 8
    packed = pl.pallas_call(
        kernel,
        out_shape=jax.ShapeDtypeStruct((BLOCK, CHUNKS, 2 * RC, 128), BF16),
        in_specs=[vmem, smem, smem, vmem, pl.BlockSpec(memory_space=pl.ANY), vmem],
        out_specs=vmem,
        scratch_shapes=[
            pltpu.VMEM((2, CHUNKS, 4, 4, 4, 2 * RC, WIDTH), BF16),
            pltpu.VMEM((4, 2, 2, PAIRS, WIDTH), BF16),
            pltpu.VMEM((2, NG, NG), BF16),
            pltpu.VMEM((2, 2 * PAIRS, NG), BF16),
            pltpu.VMEM((NQ, 2, NG, WIDTH), BF16),
            pltpu.VMEM((NQ, 4 * PAIRS, WIDTH), BF16),
            pltpu.VMEM((NQ, 4 * PAIRS, WIDTH), BF16),
            pltpu.VMEM((2, NQ, NKR, RC, 128), F32),
            pltpu.VMEM((CHUNKS, 2, BLOCK, 2, RC, 128), F32),
            pltpu.VMEM((CHUNKS, 2, BLOCK, 2, RC, 128), F32),
            pltpu.VMEM((BLOCK, 2, RC, 128), F32),
            pltpu.VMEM((CHUNKS, BLOCK, 2, RC, 128), F32),
            pltpu.VMEM((CHUNKS, BLOCK, 2 * RC, 128), BF16),
            pltpu.VMEM((CHUNKS, BLOCK, 2 * RC, 128), BF16),
            dma, dma((3,)), dma((3,)), dma((3, 3)), dma((3, 3)),
        ] + ring_sems + [dma((CHUNKS, 2)), dma((CHUNKS, 2)), dma((CHUNKS,)), dma((CHUNKS,))],
        compiler_params=pltpu.CompilerParams(
            collective_id=0, has_side_effects=True, vmem_limit_bytes=56 << 20),
    )(density, partner, qindex, gshift, screened, coulomb.reshape(1, WIDTH))
    parts = packed.reshape(BLOCK, CHUNKS, 2, RC, 2, PAIRS)
    return parts.transpose(0, 2, 4, 5, 1, 3).reshape(BLOCK, 2, 2, PAIRS * PAIRS)


def solution(mesh):
    return jax.shard_map(
        on_device,
        mesh=mesh,
        in_specs=(
            P("ka", None, None, "ga"),
            P(),
            P("ka", None),
            P("ka", None),
            P(None, None, None, "ga"),
            P("ga"),
        ),
        out_specs=P("ga", "ka", None, None),
        check_vma=False,
    )
```

time: 797 us -> 120 us (0.15)
  waiting for transfers between devices: 330 us -> 0 us
  blocking collectives: 300 us -> 0 us
  Pallas kernels: 0 us -> 102 us
  local copies, waits for them, and re-layouts: 71.9 us -> 15.9 us
  other arithmetic: 47.3 us -> 0 us
  matrix products: 27.7 us -> 0 us
  between operations: 14.2 us -> 0.02 us
    all_gather x1 -> x0, waiting for transfers between devices: 329 us -> none  [on_device(): initials = lax.all_gather(density, 'ka', axis=0, tiled=True)]
    unnamed x1 -> x0, blocking collectives: 279 us -> none
    pallas_call x0 -> x1, Pallas kernels: none -> 102 us  [on_device(): pl.pallas_call(kernel, out_shape=jax.ShapeDtypeStruct((BLOCK, CHUNKS, 2 *...]
    gather x5 -> x0, local copies, waits for them, and re-layouts: 32.3 us -> none  [the longest x2 13.1 us: contract_rows(): chosen = jnp.take(kernel[row], qcols[row], axis=0)]
    dot_general x3 -> x0, matrix products: 27.7 us -> none  [the longest x2 21.9 us: contract_rows(): jnp.einsum('jcpg,jdrg->jcdpr', chosen, cols, preferred_element_type=jnp.f...]
    sub x3 -> x0, other arithmetic: 24.3 us -> none  [the longest x2 24.2 us: contract_rows(): b_re = block[:, 0, 0] - block[:, 1, 1]]
    all_gather x1 -> x0, blocking collectives: 21.3 us -> none  [on_device(): whole_rows = lax.all_gather(density, 'ga', axis=3, tiled=True)]
    reshape x0 -> x3, local copies, waits for them, and re-layouts: none -> 15.9 us  [the longest x2 10.2 us: on_device(): parts = packed.reshape(BLOCK, CHUNKS, 2, RC, 2, PAIRS)]
  transfers between devices with their start and end apart: 1 -> 0, of which waited for: 1 -> 0; matrix products, arithmetic and copies ran while one was open for 4% -> 0% of each run, Pallas kernels for 0% -> 0%
where the time goes in v1:
time: 120 us; the launch traced here: 117 us
  Pallas kernels  102 us (85%)
  local copies, waits for them, and re-layouts  15.9 us (13%)
    pallas_call x1, Pallas kernels, on_device(): pl.pallas_call(kernel, out_shape=jax.ShapeDtypeStruct((BLOCK, CHUNKS, 2 *...  102 us
    reshape x2, local copies, waits for them, and re-layouts, on_device(): parts = packed.reshape(BLOCK, CHUNKS, 2, RC, 2, PAIRS)  10.2 us
    reshape x1, local copies, waits for them, and re-layouts, on_device(): return parts.transpose(0, 2, 4, 5, 1, 3).reshape(BLOCK, 2, 2, PAIRS * PAIRS)  5.62 us

profile of v1, /device:TPU:32, one launch (start us, length us, event | category | flops | bytes accessed | tf_op | source)
XLA Modules:
  0.0 117.4 jit_solution(16055778841696784920)
XLA Ops:
  0.0 101.5 %shard_map.64 = bf16[32,8,16,128]{3,2,1,0:T(8,128)(2,1)} custom-call(bf16[2,2,64,256]{3,2,1,0:T(8,128)(2,1)} %density.1, s32[128]{0:T(128)} %partner.1, s32[2,128]{1,0:T(2,128)} %qindex.1, s32[2,1024]{1,0:T(2,128)} %gshift.1, bf16[8,2,1024,256]{3,2,1,0:T(8,128)(2,1)} %screened.1, f32[1,256]{1,0:T(1,128)} %bitcast.7), custom_call_target="tpu_custom_call" | custom-call | tf_op jit(solution)/shard_map/pallas_call | solution.py:326
  101.6 3.9 %reshape.10 = bf16[32,8,2,8,2,64]{5,4,3,2,1,0:T(2,128)(2,1)S(1)} reshape(bf16[32,8,16,128]{3,2,1,0:T(8,128)(2,1)} %shard_map.64) | data formatting | bytes 2097152 | tf_op jit(solution)/shard_map/reshape | solution.py:351
  105.4 6.4 %copy.8 = bf16[32,8,2,8,2,64]{0,3,1,5,4,2:T(8,128)(2,1)} copy(bf16[32,8,2,8,2,64]{5,4,3,2,1,0:T(2,128)(2,1)S(1)} %reshape.10) | data formatting | bytes 2097152 | tf_op jit(solution)/shard_map/reshape | solution.py:351
  111.8 5.6 %copy.9 = bf16[32,2,2,4096]{3,2,1,0:T(2,128)(2,1)} copy(bf16[32,2,2,4096]{0,3,2,1:T(8,128)(2,1)} %bitcast.6) | data formatting | bytes 2097152 | tf_op jit(solution)/shard_map/reshape | solution.py:352

commit v2 on v1

v2 whole, which is shorter than its diff:
```python
import functools

import jax
import jax.numpy as jnp
from jax import lax
from jax.experimental import pallas as pl
from jax.experimental.pallas import tpu as pltpu
from jax.sharding import PartitionSpec as P

MESH = pl.DeviceIdType.MESH
F32, BF16 = jnp.float32, jnp.bfloat16
PAIRS, NG, NQ, NKR, WIDTH = 64, 1024, 8, 128, 256
CHUNKS = 8
RC = PAIRS // CHUNKS
BLOCK = NKR // 4
GROUPS = ((0, 2), (2, 4), (4, 6), (6, 8))
DIRECT = 1
SLABS = 4
SLAB = BLOCK // SLABS
NT = (((1,), (1,)), ((), ()))


def dot(a, b):
    return jnp.dot(a, b, preferred_element_type=F32)


def dot_nt(a, b):
    return lax.dot_general(a, b, NT, preferred_element_type=F32)


def kernel(density, partner, qindex, gshift, screened, coulomb, out,
           D, SG, OH, SH, W, KA, KB, res, xsend, xrecv, keepx, fin, csend, crecv, obuf,
           wsem, out_sem, s_r, z_r, a1_r, a2_r, b1_r, b2_r, x_r, c_r, l_r, osem):
    ka, ga = lax.axis_index("ka"), lax.axis_index("ga")
    y, x, z = ka // 16, (ka // 4) % 4, ka % 4
    half, core = ga // 2, ga % 2
    ym, yp, yo = (y + 3) % 4, (y + 1) % 4, (y + 2) % 4
    xm, xp, xo = (x + 3) % 4, (x + 1) % 4, (x + 2) % 4

    def at(yy, xx, zz):
        return (yy * 16 + xx * 4 + zz, ga)

    mate_ga = half * 2 + (1 - core)
    cross_ga = (1 - half) * 2 + core
    far_ga = (1 - half) * 2 + (1 - core)
    mate, cross = (ka, mate_ga), (ka, cross_ga)
    line = [at(y, x, (z + d) % 4) for d in (1, 2, 3)]
    ring = [at(y, xp, z), at(y, xm, z), at(yp, x, z), at(ym, x, z)]
    ring_b = [ring[2], ring[3], ring[0], ring[1]]
    opposite = [at(y, xo, z), at(yo, x, z)]

    def rc(src, dst, ss, rs, dev):
        return pltpu.make_async_remote_copy(
            src_ref=src, dst_ref=dst, send_sem=ss, recv_sem=rs, device_id=dev, device_id_type=MESH)

    z_s, a1_s, a2_s, b1_s, b2_s, s_s, x_s, c_s = (out_sem.at[i] for i in range(8))

    def got(whole, rs):
        rc(whole, whole, z_s, rs, mate).wait_recv()

    def sent(whole, ss):
        rc(whole, whole, ss, s_r.at[0], mate).wait_send()

    barrier = pltpu.get_barrier_semaphore()
    for peer in line + ring + opposite + [mate, cross]:
        pl.semaphore_signal(barrier, inc=1, device_id=peer, device_id_type=MESH)
    wcopy = pltpu.make_async_copy(screened, W, wsem)
    wcopy.start()

    for h in range(2):
        both = [density[j, h].astype(F32).reshape(CHUNKS, RC, WIDTH) for j in range(2)]
        D[h, :, y, x, z] = jnp.concatenate(both, axis=1).astype(BF16)
    SG[ga] = density[...]
    pl.semaphore_wait(barrier, 11)

    s_parts = [(SG.at[ga], mate), (SG.at[ga], cross), (SG.at[cross_ga], mate)]
    s_land = [SG.at[mate_ga], SG.at[cross_ga], SG.at[far_ga]]

    def s_send(i):
        rc(s_parts[i][0], s_parts[i][0], s_s, s_r.at[i], s_parts[i][1]).start()

    def s_got(i):
        got(s_land[i], s_r.at[i])

    def z_send(g):
        lo, hi = GROUPS[g]
        part = D.at[:, lo:hi, y, x, z]
        for d in range(3):
            rc(part, part, z_s, z_r.at[g], line[d]).start()

    def z_got(g):
        lo, hi = GROUPS[g]
        got(D.at[:, lo:hi, 0, 0, 0:3], z_r.at[g])

    def span(g):
        return pl.ds(GROUPS[g][0], GROUPS[g][1] - GROUPS[g][0])

    def send_all(parts, ss, rs, to):
        for part, dev in zip(parts, to):
            rc(part, part, ss, rs, dev).start()


    def send(name, c):
        if name == "a1":
            w = span(c)
            parts = [D.at[0, w, y, x], D.at[0, w, y, x], D.at[1, w, y, x], D.at[1, w, y, x]]
            send_all(parts, a1_s, a1_r.at[c], ring)
            if c == 0:
                send_all(parts[1:3], z_s, a1_r.at[c], opposite)
        if name == "a2":
            w = span(c)
            parts = [D.at[0, w, y, xm, 0:2], D.at[0, w, y, xp, 2:4], D.at[1, w, ym, x, 0:2], D.at[1, w, yp, x, 2:4]]
            send_all(parts, a2_s, a2_r.at[c], ring)
        if name == "b1":
            parts = [D.at[0, c, y], D.at[0, c, y], D.at[1, c, :, x], D.at[1, c, :, x]]
            send_all(parts, b1_s, b1_r.at[c], ring_b)
            if isinstance(c, int) and c < DIRECT:
                send_all(parts[1:3], b2_s, b1_r.at[c], opposite[::-1])
        if name == "b2":
            parts = [D.at[0, c, ym, 0:2], D.at[0, c, yp, 2:4], D.at[1, c, 0:2, xm], D.at[1, c, 2:4, xp]]
            send_all(parts, b2_s, b2_r.at[c], ring_b)

    def recv(name, c):
        if name == "a1":
            got(D.at[:, span(c), 0, 0:3] if c == 0 else D.at[0, span(c), 0], a1_r.at[c])
        if name == "a2":
            got(D.at[0, span(c), 0, 0:2], a2_r.at[c])
        if name == "b1":
            got(D.at[:, c, 0:3] if isinstance(c, int) and c < DIRECT else D.at[0, c], b1_r.at[c])
        if name == "b2":
            got(D.at[0, c, 0:2], b2_r.at[c])

    def shift_part(b, first):
        rows = pl.ds(pl.multiple_of(b * WIDTH, WIDTH), WIDTH)
        for j in range(2):
            term = dot(SG[b, j].reshape(2 * PAIRS, WIDTH), OH[j, rows, :])
            if first:
                SH[j] = term.astype(BF16)
            else:
                SH[j] = (SH[j].astype(F32) + term).astype(BF16)

    z_send(0)

    def build(t, _):
        rows = pl.ds(pl.multiple_of(t * 64, 64), 64)
        index = lax.broadcasted_iota(jnp.int32, (64, NG), 0) + t * 64
        for j in range(2):
            OH[j, rows, :] = jnp.where(index == gshift[j:j + 1, :], 1.0, 0.0).astype(BF16)
        return 0

    lax.fori_loop(0, NG // 64, build, 0)
    s_send(1)
    s_send(0)
    shift_part(ga, True)

    local = pl.ds(pl.multiple_of(ga * WIDTH, WIDTH), WIDTH)

    def screen(q, _):
        rows = SH[...].reshape(4 * PAIRS, NG)
        by_re, by_im = dot(rows, W[q, 0]), dot(rows, W[q, 1])
        twice = 2.0 * coulomb[...]
        a, b = [], []
        for j in range(2):
            re, im = slice(j * 128, j * 128 + 64), slice(j * 128 + 64, j * 128 + 128)
            own = SH[j, :, local].astype(F32)
            k_re = (twice * own[:64] - (by_re[re] - by_im[im])).astype(BF16)
            k_im = (twice * own[64:] - (by_im[re] + by_re[im])).astype(BF16)
            a += [k_re, k_im]
            b += [k_im, -k_re]
        KA[q] = jnp.concatenate(a, axis=0)
        KB[q] = jnp.concatenate(b, axis=0)
        return 0

    local = pl.ds(pl.multiple_of(ga * WIDTH, WIDTH), WIDTH)

    def screen(q, _):
        rows = SH[...].reshape(4 * PAIRS, NG)
        by_re, by_im = dot(rows, W[q, 0]), dot(rows, W[q, 1])
        twice = 2.0 * coulomb[...]
        a, b = [], []
        for j in range(2):
            re, im = slice(j * 128, j * 128 + 64), slice(j * 128 + 64, j * 128 + 128)
            own = SH[j, :, local].astype(F32)
            k_re = (twice * own[:64] - (by_re[re] - by_im[im])).astype(BF16)
            k_im = (twice * own[64:] - (by_im[re] + by_re[im])).astype(BF16)
            a += [k_re, k_im]
            b += [k_im, -k_re]
        KA[q] = jnp.concatenate(a, axis=0)
        KB[q] = jnp.concatenate(b, axis=0)
        return 0

    z_got(0)
    send("a1", 0)
    s_got(0)
    shift_part(mate_ga, False)
    recv("a1", 0)
    send("b1", 0)
    s_got(1)
    s_send(2)
    send("b1", 1)
    z_send(1)
    z_send(2)
    z_send(3)
    shift_part(cross_ga, False)
    s_got(2)
    shift_part(far_ga, False)
    wcopy.wait()
    lax.fori_loop(0, 5, screen, 0)
    z_got(1)
    send("a1", 1)
    lax.fori_loop(5, NQ, screen, 0)

    def multiply(c, q_lo, q_hi):
        def one(q, _):
            for t in range(4):
                d_re = D[0, c, t].reshape(256, WIDTH)
                d_im = D[1, c, t].reshape(256, WIDTH)
                both = dot_nt(d_re, KA[q]) + dot_nt(d_im, KB[q])
                for k in range(2):
                    res[k, q, t * 32:(t + 1) * 32] = both[:, k * 128:(k + 1) * 128].reshape(32, RC, 128)
            return 0

        lax.fori_loop(q_lo, q_hi, one, 0)

    def pick(block, put):
        def one(i, _):
            col = block * BLOCK + i
            m = partner[col]
            for k in range(2):
                put(i, k, res[k, qindex[k, col], m])
            return 0

        lax.fori_loop(0, BLOCK, one, 0, unroll=4)

    def x_send(c, part):
        rc(xsend.at[c, part], xrecv.at[c, part], x_s, x_r.at[c, part], mate).start()

    def x_got(c, part):
        got(xrecv.at[c, part], x_r.at[c, part])

    def c_send(c):
        x_got(c, 0)
        for part in range(SLABS):
            piece = pl.ds(part * SLAB, SLAB)
            total = keepx[piece] + xrecv[c, 0, piece]
            csend[c, part] = total.reshape(SLAB, 2 * RC, 128).astype(BF16)
            arrived = l_r.at[part] if isinstance(c, int) and c == CHUNKS - 1 else c_r.at[c]
            rc(csend.at[c, part], crecv.at[c, part], c_s, arrived, cross).start()

    def settle(c):
        rows = pl.ds(pl.multiple_of(c * RC, RC), RC)

        def put_far(i, k, v):
            xsend[c, 0, i, k] = v

        def put_mate(i, k, v):
            xsend[c, 1, i, k] = v

        def put_cross(i, k, v):
            keepx[i, k] = v

        def put_own(i, k, v):
            fin[i, k, rows] = v

        pick(far_ga, put_far)
        x_send(c, 0)
        pick(cross_ga, put_cross)
        pick(mate_ga, put_mate)
        x_send(c, 1)
        pick(ga, put_own)

    def finish(c, part):
        rows = pl.ds(pl.multiple_of(c * RC, RC), RC)
        piece = pl.ds(part * SLAB, SLAB)
        theirs = crecv[c, part].astype(F32).reshape(SLAB, 2, RC, 128)
        fin[piece, :, rows] = fin[piece, :, rows] + xrecv[c, 1, piece] + theirs

    def turn(part):
        slot = lax.broadcasted_iota(jnp.int32, (PAIRS, 128), 0)
        pair = lax.broadcasted_iota(jnp.int32, (PAIRS, 128), 1)
        same = (slot % 2 == pair // PAIRS) & (slot // 2 == (pair % PAIRS) // 2)
        chosen = jnp.where(same, 1.0, 0.0).astype(BF16)
        even = pair % 2 == 0

        def one(i, _):
            parts = []
            for k in range(2):
                t = fin[i, k].astype(BF16)
                zero = jnp.zeros_like(t)
                parts += [jnp.where(even, t, zero), jnp.where(even, zero, t)]
            turned = dot_nt(chosen, jnp.concatenate(parts, axis=0)).astype(BF16)
            obuf[i, 0] = turned[:, :128]
            obuf[i, 1] = turned[:, 128:]
            return 0

        lax.fori_loop(part * SLAB, (part + 1) * SLAB, one, 0, unroll=4)

    def o_copy(part):
        piece = pl.ds(part * SLAB, SLAB)
        return pltpu.make_async_copy(obuf.at[piece], out.at[piece], osem.at[part])

    recv("b1", 0)
    multiply(0, 0, 2)
    recv("b1", 1)
    send("b2", 1)
    recv("a1", 1)
    send("a2", 1)
    z_got(2)
    send("a1", 2)
    multiply(0, 2, 6)
    recv("a2", 1)
    send("b1", 2)
    send("b1", 3)
    z_got(3)
    send("a1", 3)
    multiply(0, 6, NQ)
    settle(0)

    recv("b2", 1)
    multiply(1, 0, NQ // 2)
    c_send(0)
    recv("b1", 2)
    send("b2", 2)
    recv("a1", 2)
    send("a2", 2)
    multiply(1, NQ // 2, NQ)
    settle(1)
    recv("a2", 2)
    send("b1", 4)
    recv("a1", 3)
    send("a2", 3)

    def tick(c, _):
        @pl.when(c + 1 < CHUNKS)
        def _():
            recv("b1", c + 1)
            send("b2", c + 1)

        @pl.when(c == 3)
        def _():
            recv("a2", 3)

        @pl.when(c + 3 < CHUNKS)
        def _():
            send("b1", c + 3)

        recv("b2", c)
        multiply(c, 0, NQ // 2)
        c_send(c - 1)
        multiply(c, NQ // 2, NQ)
        settle(c)
        return 0

    lax.fori_loop(2, CHUNKS, tick, 0)
    c_send(CHUNKS - 1)

    def rest(c, _):
        x_got(c, 1)
        return 0

    lax.fori_loop(0, CHUNKS, rest, 0)
    sent(D.at[0, 0], z_s)
    sent(D.at[0, 0:2], a1_s)
    sent(D.at[0, 0, 0:3], a2_s)
    sent(D.at[0], b1_s)
    sent(D.at[0, 0:4], b2_s)
    sent(SG.at[0:3], s_s)
    sent(xsend, x_s)

    def ends(c, _):
        got(crecv.at[c], c_r.at[c])
        for part in range(SLABS):
            finish(c, part)
        return 0

    lax.fori_loop(0, CHUNKS - 1, ends, 0)
    for part in range(SLABS):
        got(crecv.at[CHUNKS - 1, part], l_r.at[part])
        finish(CHUNKS - 1, part)
        turn(part)
        o_copy(part).start()
    sent(csend, c_s)
    for part in range(SLABS):
        o_copy(part).wait()


def move(src, dst):
    dst[...] = src[...]


def on_device(density, partner, qindex, gshift, screened, coulomb):
    vmem = pl.BlockSpec(memory_space=pltpu.VMEM)
    smem = pl.BlockSpec(memory_space=pltpu.SMEM)
    dma = pltpu.SemaphoreType.DMA
    packed = pl.pallas_call(
        kernel,
        out_shape=jax.ShapeDtypeStruct((BLOCK, 2, PAIRS, 128), BF16),
        in_specs=[vmem, smem, smem, vmem, pl.BlockSpec(memory_space=pl.ANY), vmem],
        out_specs=pl.BlockSpec(memory_space=pl.ANY),
        scratch_shapes=[
            pltpu.VMEM((2, CHUNKS, 4, 4, 4, 2 * RC, WIDTH), BF16),
            pltpu.VMEM((4, 2, 2, PAIRS, WIDTH), BF16),
            pltpu.VMEM((2, NG, NG), BF16),
            pltpu.VMEM((2, 2 * PAIRS, NG), BF16),
            pltpu.VMEM((NQ, 2, NG, WIDTH), BF16),
            pltpu.VMEM((NQ, 4 * PAIRS, WIDTH), BF16),
            pltpu.VMEM((NQ, 4 * PAIRS, WIDTH), BF16),
            pltpu.VMEM((2, NQ, NKR, RC, 128), F32),
            pltpu.VMEM((CHUNKS, 2, BLOCK, 2, RC, 128), F32),
            pltpu.VMEM((CHUNKS, 2, BLOCK, 2, RC, 128), F32),
            pltpu.VMEM((BLOCK, 2, RC, 128), F32),
            pltpu.VMEM((BLOCK, 2, PAIRS, 128), F32),
            pltpu.VMEM((CHUNKS, SLABS, SLAB, 2 * RC, 128), BF16),
            pltpu.VMEM((CHUNKS, SLABS, SLAB, 2 * RC, 128), BF16),
            pltpu.VMEM((BLOCK, 2, PAIRS, 128), BF16),
            dma, dma((8,)), dma((3,)), dma((len(GROUPS),)), dma((len(GROUPS),)), dma((len(GROUPS),)),
            dma((CHUNKS,)), dma((CHUNKS,)), dma((CHUNKS, 2)), dma((CHUNKS,)), dma((SLABS,)), dma((SLABS,)),
        ],
        compiler_params=pltpu.CompilerParams(
            collective_id=0, has_side_effects=True, vmem_limit_bytes=56 << 20),
    )(density, partner, qindex, gshift, screened, coulomb.reshape(1, WIDTH))
    packed = pl.pallas_call(
        move,
        out_shape=jax.ShapeDtypeStruct(packed.shape, packed.dtype),
        in_specs=[vmem],
        out_specs=vmem,
    )(packed)
    rows = packed.reshape(BLOCK, 2, PAIRS // 2, 2, 2 * PAIRS)
    return rows.transpose(0, 1, 3, 2, 4).reshape(BLOCK, 2, 2, PAIRS * PAIRS)


def solution(mesh):
    return jax.shard_map(
        on_device,
        mesh=mesh,
        in_specs=(
            P("ka", None, None, "ga"),
            P(),
            P("ka", None),
            P("ka", None),
            P(None, None, None, "ga"),
            P("ga"),
        ),
        out_specs=P("ga", "ka", None, None),
        check_vma=False,
    )
```

time: 120 us -> 95.7 us (0.80); the launches traced: 117 us -> 94.7 us
  local copies, waits for them, and re-layouts: 15.9 us -> 0 us
  Pallas kernels: 102 us -> 94.7 us
    reshape x3 -> x0, local copies, waits for them, and re-layouts: 15.9 us -> none  [the longest x2 10.2 us: on_device(): parts = packed.reshape(BLOCK, CHUNKS, 2, RC, 2, PAIRS)]
    pallas_call x1 -> x2, Pallas kernels: 102 us -> 94.7 us  [the longest x1 92.5 us: on_device(): pl.pallas_call(kernel, out_shape=jax.ShapeDtypeStruct((BLOCK, 2, PAIRS, 1...]
where the time goes in v2:
time: 95.7 us; the launch traced here: 94.7 us
  Pallas kernels  94.7 us (99%)
    pallas_call x1, Pallas kernels, on_device(): pl.pallas_call(kernel, out_shape=jax.ShapeDtypeStruct((BLOCK, 2, PAIRS, 1...  92.5 us
    pallas_call x1, Pallas kernels, on_device(): pl.pallas_call(move, out_shape=jax.ShapeDtypeStruct(packed.shape, packed....  2.26 us

profile of v2, /device:TPU:32, one launch (start us, length us, event | category | flops | bytes accessed | tf_op | source)
XLA Modules:
  0.0 94.7 jit_solution(11731386826828831436)
XLA Ops:
  0.0 92.5 %shard_map.64.src = bf16[32,2,64,128]{3,2,1,0:T(8,128)(2,1)} custom-call(bf16[2,2,64,256]{3,2,1,0:T(8,128)(2,1)} %density.1, s32[128]{0:T(128)} %partner.1, s32[2,128]{1,0:T(2,128)} %qindex.1, s32[2,1024]{1,0:T(2,128)} %gshift.1, bf16[8,2,1024,256]{3,2,1,0:T(8,128)(2,1)} %screened.1, f32[1,256]{1,0:T(1,128)} %bitcast.6), custom_call_target="tpu_custom_call" | custom-call | tf_op jit(solution)/shard_map/pallas_call | solution.py:395
  92.5 2.3 %shard_map.65 = bf16[32,2,64,128]{3,2,1,0:T(8,128)(2,1)} custom-call(bf16[32,2,64,128]{3,2,1,0:T(8,128)(2,1)} %shard_map.64.src), custom_call_target="tpu_custom_call" | custom-call | tf_op jit(solution)/shard_map/pallas_call | solution.py:422

commit v3 on v2

--- a/solution.py
+++ b/solution.py
@@ -230,7 +230,7 @@
                 put(i, k, res[k, qindex[k, col], m])
             return 0
 
-        lax.fori_loop(0, BLOCK, one, 0, unroll=4)
+        lax.fori_loop(0, BLOCK, one, 0, unroll=8)
 
     def x_send(c, part):
         rc(xsend.at[c, part], xrecv.at[c, part], x_s, x_r.at[c, part], mate).start()
@@ -422,8 +422,9 @@
     packed = pl.pallas_call(
         move,
         out_shape=jax.ShapeDtypeStruct(packed.shape, packed.dtype),
-        in_specs=[vmem],
-        out_specs=vmem,
+        grid=(2,),
+        in_specs=[pl.BlockSpec((BLOCK // 2, 2, PAIRS, 128), lambda i: (i, 0, 0, 0))],
+        out_specs=pl.BlockSpec((BLOCK // 2, 2, PAIRS, 128), lambda i: (i, 0, 0, 0)),
     )(packed)
     rows = packed.reshape(BLOCK, 2, PAIRS // 2, 2, 2 * PAIRS)
     return rows.transpose(0, 1, 3, 2, 4).reshape(BLOCK, 2, 2, PAIRS * PAIRS)

time: 95.7 us -> 96.2 us (level)
  Pallas kernels: 94.7 us -> 96.1 us
    pallas_call x1, Pallas kernels: 92.5 us -> 94 us  [on_device(): pl.pallas_call(kernel, out_shape=jax.ShapeDtypeStruct((BLOCK, 2, PAIRS, 1...]
where the time goes in v3:
time: 96.2 us; the launch traced here: 96.1 us
  Pallas kernels  96.1 us (100%)
    pallas_call x1, Pallas kernels, on_device(): pl.pallas_call(kernel, out_shape=jax.ShapeDtypeStruct((BLOCK, 2, PAIRS, 1...  94 us
    pallas_call x1, Pallas kernels, on_device(): pl.pallas_call(move, out_shape=jax.ShapeDtypeStruct(packed.shape, packed....  2.05 us

profile of v3, /device:TPU:32, one launch (start us, length us, event | category | flops | bytes accessed | tf_op | source)
XLA Modules:
  0.0 96.1 jit_solution(13119085575668592590)
XLA Ops:
  0.0 94.0 %shard_map.64.src = bf16[32,2,64,128]{3,2,1,0:T(8,128)(2,1)} custom-call(bf16[2,2,64,256]{3,2,1,0:T(8,128)(2,1)} %density.1, s32[128]{0:T(128)} %partner.1, s32[2,128]{1,0:T(2,128)} %qindex.1, s32[2,1024]{1,0:T(2,128)} %gshift.1, bf16[8,2,1024,256]{3,2,1,0:T(8,128)(2,1)} %screened.1, f32[1,256]{1,0:T(1,128)} %bitcast.6), custom_call_target="tpu_custom_call" | custom-call | tf_op jit(solution)/shard_map/pallas_call | solution.py:395
  94.1 2.1 %shard_map.65 = bf16[32,2,64,128]{3,2,1,0:T(8,128)(2,1)} custom-call(bf16[32,2,64,128]{3,2,1,0:T(8,128)(2,1)} %shard_map.64.src), custom_call_target="tpu_custom_call" | custom-call | tf_op jit(solution)/shard_map/pallas_call | solution.py:422

commit v4 on v3

--- a/solution.py
+++ b/solution.py
@@ -167,8 +167,8 @@
             k_im = (twice * own[64:] - (by_im[re] + by_re[im])).astype(BF16)
             a += [k_re, k_im]
             b += [k_im, -k_re]
-        KA[q] = jnp.concatenate(a, axis=0)
-        KB[q] = jnp.concatenate(b, axis=0)
+        KA[q] = jnp.concatenate(a, axis=0).T
+        KB[q] = jnp.concatenate(b, axis=0).T
         return 0
 
     local = pl.ds(pl.multiple_of(ga * WIDTH, WIDTH), WIDTH)
@@ -185,8 +185,8 @@
             k_im = (twice * own[64:] - (by_im[re] + by_re[im])).astype(BF16)
             a += [k_re, k_im]
             b += [k_im, -k_re]
-        KA[q] = jnp.concatenate(a, axis=0)
-        KB[q] = jnp.concatenate(b, axis=0)
+        KA[q] = jnp.concatenate(a, axis=0).T
+        KB[q] = jnp.concatenate(b, axis=0).T
         return 0
 
     z_got(0)
@@ -215,7 +215,7 @@
             for t in range(4):
                 d_re = D[0, c, t].reshape(256, WIDTH)
                 d_im = D[1, c, t].reshape(256, WIDTH)
-                both = dot_nt(d_re, KA[q]) + dot_nt(d_im, KB[q])
+                both = dot(d_re, KA[q]) + dot(d_im, KB[q])
                 for k in range(2):
                     res[k, q, t * 32:(t + 1) * 32] = both[:, k * 128:(k + 1) * 128].reshape(32, RC, 128)
             return 0

time: 96.2 us -> 96.2 us (level)
  no operation moved by 1% of the time
where the time goes in v4:
time: 96.2 us; the launch traced here: 96.1 us
  Pallas kernels  96.1 us (100%)
    pallas_call x1, Pallas kernels, on_device(): pl.pallas_call(kernel, out_shape=jax.ShapeDtypeStruct((BLOCK, 2, PAIRS, 1...  94 us
    pallas_call x1, Pallas kernels, on_device(): pl.pallas_call(move, out_shape=jax.ShapeDtypeStruct(packed.shape, packed....  2.05 us

profile of v4, /device:TPU:32, one launch (start us, length us, event | category | flops | bytes accessed | tf_op | source)
XLA Modules:
  0.0 96.1 jit_solution(3911167965706531563)
XLA Ops:
  0.0 94.0 %shard_map.64.src = bf16[32,2,64,128]{3,2,1,0:T(8,128)(2,1)} custom-call(bf16[2,2,64,256]{3,2,1,0:T(8,128)(2,1)} %density.1, s32[128]{0:T(128)} %partner.1, s32[2,128]{1,0:T(2,128)} %qindex.1, s32[2,1024]{1,0:T(2,128)} %gshift.1, bf16[8,2,1024,256]{3,2,1,0:T(8,128)(2,1)} %screened.1, f32[1,256]{1,0:T(1,128)} %bitcast.6), custom_call_target="tpu_custom_call" | custom-call | tf_op jit(solution)/shard_map/pallas_call | solution.py:395
  94.0 2.1 %shard_map.65 = bf16[32,2,64,128]{3,2,1,0:T(8,128)(2,1)} custom-call(bf16[32,2,64,128]{3,2,1,0:T(8,128)(2,1)} %shard_map.64.src), custom_call_target="tpu_custom_call" | custom-call | tf_op jit(solution)/shard_map/pallas_call | solution.py:422
